TPU v7x, 32 devices: a whole 2x2x4 slice. The times are simulated.
32 devices in a mesh: narrow: 2 (over x), wide: 16 (over z, y, core).
Axes of the slice: x: 2, y: 2, z: 4, core: 2. Of those that a mesh axis runs over, the one named last changes fastest.
Arguments:
- snapshots: float32 [512, 128, 1024], P('narrow', 'wide'), as said below
- start_basis: float32 [512, 64], replicated, may hold values from -6 to 6
Outputs:
- core_part: float32 [64, 128, 1024], P('narrow', 'wide')
Inputs may be any that keep to these rules, and one draw needn't show every extreme that they name: `snapshots`: real values; the x fibres have a dominant subspace of dimension 64.
All inputs are finite; a program needn't handle non-finite values.
Results may differ from a plain program's by a relative error of at most 0.0003.
Values sent between devices are 32-bit elements; how exact they have to be, the bound alone decides.
A program may use at most 64 MiB of HBM per device.

v0:
```python
import jax
import jax.numpy as jnp
from jax import lax
from jax.sharding import PartitionSpec as P

ITERS = 3


def refine_basis(factor, start_basis):
    column_basis = start_basis
    for sweep in range(ITERS):
        inner = jnp.dot(factor.T, column_basis, precision=lax.Precision.HIGHEST)
        image_cols = jnp.dot(factor, inner, precision=lax.Precision.HIGHEST)
        small_gram = jnp.dot(image_cols.T, image_cols, precision=lax.Precision.HIGHEST)
        chol_small = jnp.linalg.cholesky(small_gram)
        column_basis = lax.linalg.triangular_solve(
            chol_small, image_cols, left_side=False, lower=True, transpose_a=True
        )
    return column_basis


def on_device(snapshots, start_basis):
    whole_x = lax.all_to_all(snapshots, "narrow", split_axis=1, concat_axis=0, tiled=True)
    height = whole_x.shape[0]
    unfolded = whole_x.reshape(height, -1)
    local_gram = jnp.dot(unfolded, unfolded.T, precision=lax.Precision.HIGHEST)
    gram_acc = lax.psum(local_gram, ("narrow", "wide"))
    factor = jnp.linalg.cholesky(gram_acc)
    column_basis = refine_basis(factor, start_basis)
    partial_core = jnp.einsum("xr,xyc->ryc", column_basis, whole_x, precision=lax.Precision.HIGHEST)
    core_part = lax.all_to_all(partial_core, "narrow", split_axis=0, concat_axis=1, tiled=True)
    return core_part


def solution(mesh):
    placed = (P("narrow", "wide", None), P())
    return jax.shard_map(
        on_device, mesh=mesh, in_specs=placed, out_specs=P("narrow", "wide", None), check_vma=False
    )
```

profile of v0, /device:TPU:0, one launch (start us, length us, event | category | flops | bytes accessed | tf_op | source)
XLA Modules:
  0.0 445.5 jit_solution(5748271500465998028)
XLA Ops:
  6.5 8.3 %copy.18 = f32[256,8,1024]{2,0,1:T(8,128)S(1)} copy(f32[256,8,1024]{2,1,0:T(8,128)} %param.5) | data formatting | bytes 16777216 | tf_op args[0]
  14.8 98.1 %all_to_all.36 = f32[256,8,1024]{2,0,1:T(8,128)} all-to-all(f32[256,8,1024]{2,0,1:T(8,128)S(1)} %copy.18), channel_id=1, replica_groups=mesh['narrow'=2,'wide'=16] {'narrow'}, dimensions={1} | all-to-all | bytes 16777216 | tf_op jit(solution)/shard_map/all_to_all | solution.py:23
  112.9 12.0 %copy.32 = f32[256,2,4,1024]{3,2,0,1:T(4,128)} copy(f32[256,2,4,1024]{3,0,2,1:T(8,128)} %bitcast.91) | data formatting | bytes 16777216 | tf_op jit(solution)/shard_map/all_to_all | solution.py:23
  124.9 11.9 %copy.29 = f32[64,8,4,1024]{3,1,2,0:T(8,128)S(1)} copy(f32[64,8,4,1024]{3,2,1,0:T(4,128)} %bitcast.88) | data formatting | bytes 16777216
  136.9 16.1 %fusion.43 = f32[512,512]{0,1:T(8,128)} fusion(f32[512,4096]{1,0:T(8,128)S(1)} %bitcast.87), kind=kOutput, calls=%fused_computation.84 | convolution fusion | flops 12884901888 | bytes 9437184 | tf_op jit(solution)/shard_map/dot_general | solution.py:26
  153.0 11.5 %copy.25 = f32[2,256,4,1024]{3,1,0,2:T(8,128)} copy(f32[2,256,4,1024]{3,2,1,0:T(4,128)} %bitcast.89) | data formatting | bytes 16777216 | tf_op jit(solution)/shard_map/all_to_all | solution.py:23
  164.5 119.0 %all-reduce.3.cloned.1.call-done = f32[512,512]{0,1:T(8,128)} async-done(((f32[512,512]{0,1:T(8,128)}), f32[512,512]{0,1:T(8,128)}) %all-reduce.3.cloned.1.call-update) | async-done | bytes 1048592 | tf_op jit(solution)/shard_map/psum | solution.py:27
  283.5 1.6 copy.21
  285.1 1.4 fusion
  286.5 11.7 %cholesky.120 = f32[128,128]{1,0:T(8,128)S(1)} custom-call(f32[128,128]{1,0:T(8,128)S(1)} %cholesky.356), custom_call_target="Cholesky" | custom-call | tf_op jit(solution)/shard_map/jit(cholesky)/cholesky | solution.py:28
  298.3 9.8 %custom-call.32 = f32[1,128,128]{1,2,0:T(8,128)S(1)} custom-call(f32[1,128,128]{2,1,0:T(8,128)S(1)} %get-tuple-element.18), custom_call_target="InvertDiagBlocksLowerTriangular" | custom-call | tf_op jit(solution)/shard_map/jit(cholesky)/cholesky | solution.py:28
  309.1 11.7 %cholesky.244 = f32[128,128]{1,0:T(8,128)S(1)} custom-call(f32[128,128]{1,0:T(8,128)S(1)} %cholesky.360), custom_call_target="Cholesky" | custom-call | tf_op jit(solution)/shard_map/jit(cholesky)/cholesky | solution.py:28
  320.8 9.8 %custom-call.33 = f32[1,128,128]{1,2,0:T(8,128)S(1)} custom-call(f32[1,128,128]{2,1,0:T(8,128)S(1)} %get-tuple-element.15), custom_call_target="InvertDiagBlocksLowerTriangular" | custom-call | tf_op jit(solution)/shard_map/jit(cholesky)/cholesky | solution.py:28
  331.3 11.7 %cholesky.265 = f32[128,128]{1,0:T(8,128)S(1)} custom-call(f32[128,128]{1,0:T(8,128)S(1)} %cholesky.365), custom_call_target="Cholesky" | custom-call | tf_op jit(solution)/shard_map/jit(cholesky)/cholesky | solution.py:28
  343.7 10.0 %custom-call.34 = f32[1,128,128]{1,2,0:T(8,128)S(1)} custom-call(f32[1,128,128]{2,1,0:T(8,128)S(1)} %get-tuple-element.12), custom_call_target="InvertDiagBlocksLowerTriangular" | custom-call | tf_op jit(solution)/shard_map/jit(cholesky)/cholesky | solution.py:28
  354.3 11.7 %cholesky.282 = f32[128,128]{1,0:T(8,128)S(1)} custom-call(f32[128,128]{1,0:T(8,128)S(1)} %convolution_subtract_fusion.2), custom_call_target="Cholesky" | custom-call | tf_op jit(solution)/shard_map/jit(cholesky)/cholesky | solution.py:28
  371.7 5.8 %cholesky.325 = f32[64,64]{1,0:T(8,128)S(1)} custom-call(f32[64,64]{1,0:T(8,128)S(1)} %fusion.26), custom_call_target="Cholesky" | custom-call | tf_op jit(solution)/shard_map/jit(cholesky)/cholesky | solution.py:15
  378.9 4.9 %custom-call.37 = f32[1,64,64]{1,2,0:T(8,128)S(1)} custom-call(f32[1,64,64]{2,1,0:T(8,128)S(1)} %fusion.18), custom_call_target="InvertDiagBlocksLowerTriangular" | custom-call | tf_op jit(solution)/shard_map/triangular_solve/custom-call.8 | solution.py:16
  386.0 5.8 %cholesky.336 = f32[64,64]{1,0:T(8,128)S(1)} custom-call(f32[64,64]{1,0:T(8,128)S(1)} %fusion.24), custom_call_target="Cholesky" | custom-call | tf_op jit(solution)/shard_map/jit(cholesky)/cholesky | solution.py:15
  393.2 4.9 %custom-call.38 = f32[1,64,64]{1,2,0:T(8,128)S(1)} custom-call(f32[1,64,64]{2,1,0:T(8,128)S(1)} %fusion.19), custom_call_target="InvertDiagBlocksLowerTriangular" | custom-call | tf_op jit(solution)/shard_map/triangular_solve/custom-call.8 | solution.py:16
  400.6 5.8 %cholesky.347 = f32[64,64]{1,0:T(8,128)S(1)} custom-call(f32[64,64]{1,0:T(8,128)S(1)} %fusion.22), custom_call_target="Cholesky" | custom-call | tf_op jit(solution)/shard_map/jit(cholesky)/cholesky | solution.py:15
  407.8 4.9 %custom-call.39 = f32[1,64,64]{1,2,0:T(8,128)S(1)} custom-call(f32[1,64,64]{2,1,0:T(8,128)S(1)} %fusion.20), custom_call_target="InvertDiagBlocksLowerTriangular" | custom-call | tf_op jit(solution)/shard_map/triangular_solve/custom-call.8 | solution.py:16
  413.1 7.5 %fusion.47 = f32[64,4,1024]{2,0,1:T(8,128)S(1)} fusion(f32[512,64,1]{0,1,2:T(8,128)S(1)} %convolution_bitcast_fusion, f32[512,4,1024]{2,0,1:T(8,128)} %bitcast.90), kind=kOutput, calls=%fused_computation.88 | convolution fusion | flops 1610612736 | bytes 9568256 | tf_op jit(solution)/shard_map/xr,xyc->ryc/dot_general | solution.py:30
  421.3 15.5 %all_to_all.37 = f32[64,4,1024]{2,1,0:T(4,128)S(1)} all-to-all(f32[64,4,1024]{2,1,0:T(4,128)S(1)} %copy.26), channel_id=1, replica_groups=mesh['narrow'=2,'wide'=16] {'narrow'}, dimensions={0} | all-to-all | bytes 2097152 | tf_op jit(solution)/shard_map/all_to_all | solution.py:31
  (51 shorter events, 17.3 us)
Async XLA Ops:
  6.5 363.2 %copy-start = (f32[512,64]{0,1:T(8,128)S(1)}, f32[512,64]{0,1:T(8,128)}, u32[]{:S(2)}) copy-start(f32[512,64]{0,1:T(8,128)} %param.6) | copy-start | bytes 393220
  6.5 277.0 %all-reduce.3.cloned.1.call-start = ((), (), s32[]{:S(2)}) async-start(), calls=%async_computation.2 | async-start | bytes 2097152 | tf_op jit(solution)/shard_map/psum | solution.py:27
Sparse Core Ops, SparseCore 0:
  153.2 130.3 all-reduce.2
where the time goes:
time: 450 us; the launch traced here: 445 us
  waiting for transfers between devices  119 us (26%)
  other arithmetic  116 us (26%)
  blocking collectives  114 us (25%)
  local copies, waits for them, and re-layouts  47.7 us (11%)
  matrix products  32.4 us (7%)
  between operations  16.6 us (4%)
    psum x1, waiting for transfers between devices, on_device(): gram_acc = lax.psum(local_gram, ('narrow', 'wide'))  119 us
    all_to_all x1, blocking collectives, on_device(): lax.all_to_all(snapshots, 'narrow', split_axis=1, concat_axis=0, tiled=True)  98.1 us
    another operation x14, other arithmetic, on_device(): factor = jnp.linalg.cholesky(gram_acc)  78.5 us
    all_to_all x2, local copies, waits for them, and re-layouts, on_device(): lax.all_to_all(snapshots, 'narrow', split_axis=1, concat_axis=0, tiled=True)  23.4 us
    unnamed x4, local copies, waits for them, and re-layouts  20.2 us
    another operation x9, other arithmetic, refine_basis(): chol_small = jnp.linalg.cholesky(small_gram)  19.6 us
    another operation x6, other arithmetic, refine_basis(): lax.linalg.triangular_solve(chol_small, image_cols, left_side=False, lowe...  16.6 us
    dot_general x1, matrix products, on_device(): local_gram = jnp.dot(unfolded, unfolded.T, precision=lax.Precision.HIGHEST)  16.1 us
  transfers between devices with their start and end apart: 1, of which 1 were waited for; matrix products, arithmetic and copies ran while one was open for 3% of the time, Pallas kernels for 0%

commit v1 on v0

v1 whole, which is shorter than its diff:
```python
import jax
import jax.numpy as jnp
from jax import lax
from jax.experimental import pallas as pl
from jax.experimental.pallas import tpu as pltpu
from jax.sharding import PartitionSpec as P

ITERS = 3
RANK = 64
MESH = pl.DeviceIdType.MESH
HIGH = lax.Precision.HIGHEST
F32 = jnp.float32
BF16 = jnp.bfloat16

WIDE = 16
HALF = 256
YS = 8
LS = 1024
LH = LS // 2
COLS = YS * LH
CHUNKS = 4
CX = HALF // CHUNKS
UNITS = 2 * CHUNKS


def dot_nt(a, b):
    return lax.dot_general(a, b, (((1,), (1,)), ((), ())), preferred_element_type=F32)


def dot_nn(a, b):
    return jnp.dot(a, b, preferred_element_type=F32)


def split(value):
    hi = value.astype(BF16)
    return hi, (value - hi.astype(F32)).astype(BF16)


def inverse_chol(gram):
    n = gram.shape[0]
    rows = lax.broadcasted_iota(jnp.int32, (n, 2 * n), 0)
    lanes = lax.broadcasted_iota(jnp.int32, (n, 2 * n), 1)
    eye = (lanes == rows + n).astype(F32)
    table = jnp.concatenate([gram, jnp.zeros((n, n), F32)], axis=1) + eye
    for k in range(n - 1):
        row = table[k : k + 1, :]
        column = jnp.broadcast_to(table[:, k : k + 1], (n, 2 * n))
        scaled = row / row[:, k : k + 1]
        table = table - jnp.where(rows > k, column, 0.0) * scaled
    pivots = jnp.sum(jnp.where(lanes == rows, table, 0.0), axis=1, keepdims=True)
    return (table * lax.rsqrt(pivots))[:, n:]


def kernel(s_hbm, start_ref, out_ref, s32, rbuf, shi, slo, rhi, rlo, stage, landed, gathered, acc,
           gram_ref, basis_ref, core_send, core_own, core_land, load_sem, x_send, x_recv, rs_send,
           rs_recv, pair_send, pair_recv, ag_send, ag_recv, core_ssem, core_rsem, own_sem, land_sem):
    n = lax.axis_index("narrow")
    w = lax.axis_index("wide")
    other = 1 - n
    partner = (other, w)

    def plane(d):
        return (n, lax.rem(w + d, WIDE))

    def loads(q):
        return pltpu.make_async_copy(s_hbm.at[:, pl.ds(q * 128, 128)], s32.at[q], load_sem.at[q])

    def send_chunk(k):
        part = pl.ds(k * CX * YS, CX * YS)
        for q in range(LH // 128):
            pltpu.make_async_remote_copy(
                src_ref=s_hbm.at[part, pl.ds(pl.multiple_of(other * LH + q * 128, 128), 128)],
                dst_ref=rbuf.at[q, part], send_sem=x_send.at[k], recv_sem=x_recv.at[k],
                device_id=partner, device_id_type=MESH).start()

    barrier = pltpu.get_barrier_semaphore()
    pl.semaphore_signal(barrier, inc=1, device_id=partner, device_id_type=MESH)

    def greet(d, carry):
        pl.semaphore_signal(barrier, inc=1, device_id=plane(d), device_id_type=MESH)
        return carry

    lax.fori_loop(1, WIDE, greet, 0)
    for q in range(LS // 128):
        loads(q).start()
    pl.semaphore_wait(barrier, WIDE)
    send_chunk(0)
    send_chunk(1)

    my_rows = pl.ds(pl.multiple_of(w * 8, 8), 8)
    gat_own = pl.ds(pl.multiple_of(n * 128 + w * 8, 8), 8)
    gat_other = pl.ds(pl.multiple_of(other * 128 + w * 8, 8), 8)

    def scatter(u):
        def one(d, carry):
            to = lax.rem(w + d, WIDE)
            pltpu.make_async_remote_copy(
                src_ref=stage.at[u, pl.ds(pl.multiple_of(to * 8, 8), 8)],
                dst_ref=landed.at[u, pl.ds(pl.multiple_of((WIDE - 1 - d) * 8, 8), 8)],
                send_sem=rs_send.at[u], recv_sem=rs_recv.at[u],
                device_id=(n, to), device_id_type=MESH).start()
            return carry

        lax.fori_loop(1, WIDE, one, 0)

    def pair_copy(u):
        return pltpu.make_async_remote_copy(
            src_ref=gathered.at[u, gat_own], dst_ref=gathered.at[u, gat_own],
            send_sem=pair_send.at[u], recv_sem=pair_recv.at[u],
            device_id=partner, device_id_type=MESH)

    def spread(u, part):
        def one(d, carry):
            pltpu.make_async_remote_copy(
                src_ref=gathered.at[u, part], dst_ref=gathered.at[u, part],
                send_sem=ag_send.at[u], recv_sem=ag_recv.at[u],
                device_id=plane(d), device_id_type=MESH).start()
            return carry

        lax.fori_loop(1, WIDE, one, 0)

    def bytes_of(ref, sem):
        return pltpu.make_async_copy(ref, ref, sem)

    fifteen = pl.ds(0, (WIDE - 1) * 8)
    thirty = pl.ds(0, 2 * (WIDE - 1) * 8)

    def reduce_own(u):
        bytes_of(landed.at[u, fifteen], rs_recv.at[u]).wait()
        total = stage[u, my_rows, :]
        for d in range(WIDE - 1):
            total = total + landed[u, pl.ds(d * 8, 8), :]
        gathered[u, gat_own, :] = total
        pair_copy(u).start()
        spread(u, gat_own)

    def forward(u):
        pair_copy(u).wait_recv()
        spread(u, gat_other)

    def finish(u):
        bytes_of(gathered.at[u, thirty], ag_recv.at[u]).wait()

    for q in range(LS // 128):
        loads(q).wait()

    def convert(y, carry):
        for q in range(LS // 128):
            hi, lo = split(s32[q, pl.ds(y, HALF, stride=YS), :])
            h, r = divmod(q * 128, LH)
            at = pl.ds(pl.multiple_of(h * COLS + y * LH + r, 128), 128)
            shi[:, at] = hi
            slo[:, at] = lo
        return carry

    lax.fori_loop(0, YS, convert, 0)

    acc[...] = jnp.zeros_like(acc)

    def diagonal(b, carry):
        at = pl.ds(pl.multiple_of(b * 1024, 1024), 1024)
        hi, lo = shi[:, at], slo[:, at]
        acc[...] += dot_nt(hi, hi) + (dot_nt(hi, lo) + dot_nt(lo, hi))
        return carry

    lax.fori_loop(0, 2 * COLS // 1024, diagonal, 0)
    for u in range(CHUNKS):
        for h in range(2):
            stage[u, pl.ds(h * CX, CX), :] = acc[pl.ds(u * CX, CX), pl.ds(h * 128, 128)]
        scatter(u)
    basis_ref[...] = start_ref[...].T
    for u in range(CHUNKS):
        reduce_own(u)
    for u in range(CHUNKS):
        forward(u)

    for k in range(CHUNKS):
        arriving = rbuf.at[:, pl.ds(k * CX * YS, CX * YS)]
        bytes_of(arriving, x_send.at[k]).wait()
        if k + 2 < CHUNKS:
            send_chunk(k + 2)
        bytes_of(arriving, x_recv.at[k]).wait()
        rows = pl.ds(k * CX, CX)
        acc[rows, :] = jnp.zeros((CX, HALF), F32)

        def arrived(y, carry):
            at = pl.ds(pl.multiple_of(y * LH, LH), LH)
            cells = pl.ds(k * CX * YS + y, CX, stride=YS)
            hi, lo = split(jnp.concatenate([rbuf[q, cells, :] for q in range(LH // 128)], axis=1))
            rhi[rows, at] = hi
            rlo[rows, at] = lo
            mine = pl.ds(pl.multiple_of(n * COLS + y * LH, LH), LH)
            ohi, olo = shi[:, mine], slo[:, mine]
            acc[rows, :] += dot_nt(hi, ohi) + (dot_nt(lo, ohi) + dot_nt(hi, olo))
            return carry

        lax.fori_loop(0, YS, arrived, 0)
        u = CHUNKS + k
        for h in range(2):
            stage[u, pl.ds(h * CX, CX), :] = acc[rows, pl.ds(h * 128, 128)]
        scatter(u)
        if k >= 1:
            reduce_own(u - 1)
            forward(u - 1)
    reduce_own(UNITS - 1)
    forward(UNITS - 1)
    for u in range(CHUNKS):
        finish(u)
        for p in range(2):
            for h in range(2):
                gram_ref[pl.ds(p * HALF + u * CX, CX), pl.ds(p * HALF + h * 128, 128)] = (
                    gathered[u, pl.ds(p * 128 + h * CX, CX), :])
    for u in range(CHUNKS, UNITS):
        finish(u)
        for p in range(2):
            for h in range(2):
                gram_ref[pl.ds((1 - p) * HALF + (u - CHUNKS) * CX, CX), pl.ds(p * HALF + h * 128, 128)] = (
                    gathered[u, pl.ds(p * 128 + h * CX, CX), :])
    lower = gram_ref[pl.ds(HALF, HALF), pl.ds(0, HALF)] + gram_ref[pl.ds(0, HALF), pl.ds(HALF, HALF)].T
    gram_ref[pl.ds(HALF, HALF), pl.ds(0, HALF)] = lower
    gram_ref[pl.ds(0, HALF), pl.ds(HALF, HALF)] = lower.T

    def sweep(i, carry):
        image = jnp.dot(basis_ref[...], gram_ref[...], precision=HIGH, preferred_element_type=F32)
        small = lax.dot_general(image, image, (((1,), (1,)), ((), ())), precision=HIGH,
                                preferred_element_type=F32)
        basis_ref[...] = jnp.dot(inverse_chol(small), image, precision=HIGH, preferred_element_type=F32)
        return carry

    lax.fori_loop(0, ITERS, sweep, 0)

    own_hi, own_lo = split(basis_ref[:, pl.ds(pl.multiple_of(n * HALF, HALF), HALF)])
    oth_hi, oth_lo = split(basis_ref[:, pl.ds(pl.multiple_of(other * HALF, HALF), HALF)])
    own_both = jnp.concatenate([own_hi, own_lo], axis=0)
    oth_both = jnp.concatenate([oth_hi, oth_lo], axis=0)
    BL = LH // 2

    def core_copy(b):
        part = pl.ds(b * (BL // 128), BL // 128)
        return pltpu.make_async_remote_copy(
            src_ref=core_send.at[part], dst_ref=core_land.at[part],
            send_sem=core_ssem.at[b], recv_sem=core_rsem.at[b],
            device_id=partner, device_id_type=MESH)

    for b in range(2):
        for y in range(YS):
            mine = pl.ds(pl.multiple_of(n * COLS + y * LH + b * BL, BL), BL)
            theirs = pl.ds(y * LH + b * BL, BL)
            both = dot_nn(own_both, shi[:, mine]) + dot_nn(oth_both, rhi[:, theirs])
            low = dot_nn(own_hi, slo[:, mine]) + dot_nn(oth_hi, rlo[:, theirs])
            res = both[:RANK] + (both[RANK:] + low)
            first, second = res[: RANK // 2], res[RANK // 2 :]
            at = pl.ds(y, RANK // 2, stride=YS)
            for q in range(BL // 128):
                lane = slice(q * 128, (q + 1) * 128)
                to = b * (BL // 128) + q
                core_own[to, at, :] = jnp.where(n == 0, first[:, lane], second[:, lane])
                core_send[to, at, :] = jnp.where(n == 0, second[:, lane], first[:, lane])
        core_copy(b).start()

    def outs(source, half, sem):
        return [pltpu.make_async_copy(
            source.at[q], out_ref.at[:, pl.ds(pl.multiple_of(half * LH + q * 128, 128), 128)], sem.at[q])
            for q in range(LH // 128)]

    own_out = outs(core_own, n, own_sem)
    for copy in own_out:
        copy.start()
    for u in range(UNITS):
        bytes_of(stage.at[u, fifteen], rs_send.at[u]).wait()
        pair_copy(u).wait_send()
        bytes_of(gathered.at[u, thirty], ag_send.at[u]).wait()
    for b in range(2):
        core_copy(b).wait_recv()
    land_out = outs(core_land, other, land_sem)
    for copy in land_out:
        copy.start()
    for b in range(2):
        core_copy(b).wait_send()
    for copy in own_out + land_out:
        copy.wait()


def in_one_kernel(snapshots, start_basis):
    rows = RANK // 2 * YS
    dma = pltpu.SemaphoreType.DMA
    out = pl.pallas_call(
        kernel,
        out_shape=jax.ShapeDtypeStruct((rows, LS), F32),
        in_specs=[pl.BlockSpec(memory_space=pl.ANY), pl.BlockSpec(memory_space=pltpu.VMEM)],
        out_specs=pl.BlockSpec(memory_space=pl.ANY),
        scratch_shapes=[
            pltpu.VMEM((LS // 128, HALF * YS, 128), F32),
            pltpu.VMEM((LH // 128, HALF * YS, 128), F32),
            pltpu.VMEM((HALF, 2 * COLS), BF16),
            pltpu.VMEM((HALF, 2 * COLS), BF16),
            pltpu.VMEM((HALF, COLS), BF16),
            pltpu.VMEM((HALF, COLS), BF16),
            pltpu.VMEM((UNITS, 128, 128), F32),
            pltpu.VMEM((UNITS, 128, 128), F32),
            pltpu.VMEM((UNITS, 256, 128), F32),
            pltpu.VMEM((HALF, HALF), F32),
            pltpu.VMEM((2 * HALF, 2 * HALF), F32),
            pltpu.VMEM((RANK, 2 * HALF), F32),
            pltpu.VMEM((LH // 128, rows, 128), F32),
            pltpu.VMEM((LH // 128, rows, 128), F32),
            pltpu.VMEM((LH // 128, rows, 128), F32),
            dma((LS // 128,)), dma((CHUNKS,)), dma((CHUNKS,)),
            dma((UNITS,)), dma((UNITS,)), dma((UNITS,)), dma((UNITS,)), dma((UNITS,)), dma((UNITS,)),
            dma((2,)), dma((2,)), dma((LH // 128,)), dma((LH // 128,)),
        ],
        compiler_params=pltpu.CompilerParams(
            collective_id=0, has_side_effects=True, vmem_limit_bytes=48 * 1024 * 1024),
    )(snapshots.reshape(HALF * YS, LS), start_basis)
    return out.reshape(RANK // 2, YS, LS)


def with_collectives(snapshots, start_basis):
    whole_x = lax.all_to_all(snapshots, "narrow", split_axis=1, concat_axis=0, tiled=True)
    unfolded = whole_x.reshape(whole_x.shape[0], -1)
    gram = lax.psum(jnp.dot(unfolded, unfolded.T, precision=HIGH), ("narrow", "wide"))
    column_basis = start_basis
    for sweep in range(ITERS):
        image_cols = jnp.dot(gram, column_basis, precision=HIGH)
        small_gram = jnp.dot(image_cols.T, image_cols, precision=HIGH)
        chol_small = jnp.linalg.cholesky(small_gram)
        column_basis = lax.linalg.triangular_solve(
            chol_small, image_cols, left_side=False, lower=True, transpose_a=True)
    partial_core = jnp.einsum("xr,xyc->ryc", column_basis, whole_x, precision=HIGH)
    return lax.all_to_all(partial_core, "narrow", split_axis=0, concat_axis=1, tiled=True)


def solution(mesh):
    whole = mesh.shape["narrow"] == 2 and mesh.shape["wide"] == WIDE
    placed = (P("narrow", "wide", None), P())
    return jax.shard_map(
        in_one_kernel if whole else with_collectives,
        mesh=mesh, in_specs=placed, out_specs=P("narrow", "wide", None), check_vma=False)
```

time: 450 us -> 158 us (0.35); the launches traced: 445 us -> 158 us
  Pallas kernels: 0 us -> 156 us
  waiting for transfers between devices: 119 us -> 0 us
  other arithmetic: 116 us -> 0 us
  blocking collectives: 114 us -> 0 us
  local copies, waits for them, and re-layouts: 47.7 us -> 2 us
  matrix products: 32.4 us -> 0 us
  between operations: 16.6 us -> 0.02 us
    pallas_call x0 -> x1, Pallas kernels: none -> 156 us  [in_one_kernel(): pl.pallas_call(kernel, out_shape=jax.ShapeDtypeStruct((rows, LS), F32), i...]
    psum x1 -> x0, waiting for transfers between devices: 119 us -> none  [on_device(): gram_acc = lax.psum(local_gram, ('narrow', 'wide'))]
    another operation x29 -> x0, other arithmetic: 115 us -> none  [the longest x14 78.5 us: on_device(): factor = jnp.linalg.cholesky(gram_acc)]
    all_to_all x2 -> x0, blocking collectives: 114 us -> none  [the longest x1 98.1 us: on_device(): lax.all_to_all(snapshots, 'narrow', split_axis=1, concat_axis=0, tiled=True)]
    dot_general x11 -> x0, matrix products: 29.3 us -> none  [the longest x1 16.1 us: on_device(): local_gram = jnp.dot(unfolded, unfolded.T, precision=lax.Precision.HIGHEST)]
    all_to_all x4 -> x0, local copies, waits for them, and re-layouts: 24.9 us -> none  [the longest x2 23.4 us: on_device(): lax.all_to_all(snapshots, 'narrow', split_axis=1, concat_axis=0, tiled=True)]
    unnamed x4 -> x2, local copies, waits for them, and re-layouts: 20.2 us -> 2 us
  transfers between devices with their start and end apart: 1 -> 0, of which waited for: 1 -> 0; matrix products, arithmetic and copies ran while one was open for 3% -> 0% of each run, Pallas kernels for 0% -> 0%
where the time goes in v1:
time: 158 us
  Pallas kernels  156 us (99%)
  local copies, waits for them, and re-layouts  2 us (1%)
    pallas_call x1, Pallas kernels, in_one_kernel(): pl.pallas_call(kernel, out_shape=jax.ShapeDtypeStruct((rows, LS), F32), i...  156 us

profile of v1, /device:TPU:0, one launch (start us, length us, event | category | flops | bytes accessed | tf_op | source)
XLA Modules:
  0.0 158.0 jit_solution(1784945256818684998)
XLA Ops:
  0.0 1.0 copy.3.start_ref
  1.0 156.0 %shard_map.28 = f32[256,1024]{1,0:T(8,128)S(1)} custom-call(f32[2048,1024]{1,0:T(8,128)} %bitcast.3, f32[512,64]{1,0:T(8,128)S(1)} %copy.3.start_ref), custom_call_target="tpu_custom_call" | custom-call | tf_op jit(solution)/shard_map/pallas_call | solution.py:287
  157.0 1.0 copy.5

commit v2 on v1

--- a/solution.py
+++ b/solution.py
@@ -7,6 +7,7 @@
 
 ITERS = 3
 RANK = 64
+BLOCK = 8
 MESH = pl.DeviceIdType.MESH
 HIGH = lax.Precision.HIGHEST
 F32 = jnp.float32
@@ -42,11 +43,18 @@
     lanes = lax.broadcasted_iota(jnp.int32, (n, 2 * n), 1)
     eye = (lanes == rows + n).astype(F32)
     table = jnp.concatenate([gram, jnp.zeros((n, n), F32)], axis=1) + eye
-    for k in range(n - 1):
-        row = table[k : k + 1, :]
-        column = jnp.broadcast_to(table[:, k : k + 1], (n, 2 * n))
-        scaled = row / row[:, k : k + 1]
-        table = table - jnp.where(rows > k, column, 0.0) * scaled
+    for k in range(0, n, BLOCK):
+        row = [table[k + i : k + i + 1, :] for i in range(BLOCK)]
+        column = [jnp.broadcast_to(table[:, k + i : k + i + 1], (n, 2 * n)) for i in range(BLOCK)]
+        inverse = []
+        for i in range(BLOCK):
+            inverse.append(1.0 / column[i][k + i : k + i + 1, :])
+            for j in range(i + 1, BLOCK):
+                ratio = column[i][k + j : k + j + 1, :] * inverse[i]
+                row[j] = row[j] - ratio * row[i]
+                column[j] = column[j] - ratio * column[i]
+        for i in range(BLOCK):
+            table = table - jnp.where(rows > k + i, column[i], 0.0) * (row[i] * inverse[i])
     pivots = jnp.sum(jnp.where(lanes == rows, table, 0.0), axis=1, keepdims=True)
     return (table * lax.rsqrt(pivots))[:, n:]
 
@@ -85,7 +93,6 @@
         loads(q).start()
     pl.semaphore_wait(barrier, WIDE)
     send_chunk(0)
-    send_chunk(1)
 
     my_rows = pl.ds(pl.multiple_of(w * 8, 8), 8)
     gat_own = pl.ds(pl.multiple_of(n * 128 + w * 8, 8), 8)
@@ -168,18 +175,17 @@
         for h in range(2):
             stage[u, pl.ds(h * CX, CX), :] = acc[pl.ds(u * CX, CX), pl.ds(h * 128, 128)]
         scatter(u)
+    send_chunk(1)
     basis_ref[...] = start_ref[...].T
     for u in range(CHUNKS):
         reduce_own(u)
-    for u in range(CHUNKS):
-        forward(u)
 
     for k in range(CHUNKS):
         arriving = rbuf.at[:, pl.ds(k * CX * YS, CX * YS)]
-        bytes_of(arriving, x_send.at[k]).wait()
-        if k + 2 < CHUNKS:
-            send_chunk(k + 2)
         bytes_of(arriving, x_recv.at[k]).wait()
+        if k == 1:
+            for u in range(CHUNKS):
+                forward(u)
         rows = pl.ds(k * CX, CX)
         acc[rows, :] = jnp.zeros((CX, HALF), F32)
 
@@ -199,10 +205,13 @@
         for h in range(2):
             stage[u, pl.ds(h * CX, CX), :] = acc[rows, pl.ds(h * 128, 128)]
         scatter(u)
-        if k >= 1:
-            reduce_own(u - 1)
+        if k == CHUNKS - 1:
             forward(u - 1)
-    reduce_own(UNITS - 1)
+        reduce_own(u)
+        if k + 2 < CHUNKS:
+            send_chunk(k + 2)
+        if 1 <= k < CHUNKS - 1:
+            forward(u - 1)
     forward(UNITS - 1)
     for u in range(CHUNKS):
         finish(u)
@@ -266,6 +275,8 @@
     own_out = outs(core_own, n, own_sem)
     for copy in own_out:
         copy.start()
+    for k in range(CHUNKS):
+        bytes_of(rbuf.at[:, pl.ds(k * CX * YS, CX * YS)], x_send.at[k]).wait()
     for u in range(UNITS):
         bytes_of(stage.at[u, fifteen], rs_send.at[u]).wait()
         pair_copy(u).wait_send()

time: 158 us -> 139 us (0.88)
  Pallas kernels: 156 us -> 137 us
    pallas_call x1, Pallas kernels: 156 us -> 137 us  [in_one_kernel(): pl.pallas_call(kernel, out_shape=jax.ShapeDtypeStruct((rows, LS), F32), i...]
where the time goes in v2:
time: 139 us
  Pallas kernels  137 us (99%)
  local copies, waits for them, and re-layouts  2 us (1%)
    pallas_call x1, Pallas kernels, in_one_kernel(): pl.pallas_call(kernel, out_shape=jax.ShapeDtypeStruct((rows, LS), F32), i...  137 us

profile of v2, /device:TPU:0, one launch (start us, length us, event | category | flops | bytes accessed | tf_op | source)
XLA Modules:
  0.0 139.3 jit_solution(6799257559598295922)
XLA Ops:
  0.0 1.0 copy.3.start_ref
  1.0 137.3 %shard_map.28 = f32[256,1024]{1,0:T(8,128)S(1)} custom-call(f32[2048,1024]{1,0:T(8,128)} %bitcast.3, f32[512,64]{1,0:T(8,128)S(1)} %copy.3.start_ref), custom_call_target="tpu_custom_call" | custom-call | tf_op jit(solution)/shard_map/pallas_call | solution.py:298
  138.3 1.0 copy.5

commit v3 on v2

--- a/solution.py
+++ b/solution.py
@@ -78,7 +78,7 @@
         for q in range(LH // 128):
             pltpu.make_async_remote_copy(
                 src_ref=s_hbm.at[part, pl.ds(pl.multiple_of(other * LH + q * 128, 128), 128)],
-                dst_ref=rbuf.at[q, part], send_sem=x_send.at[k], recv_sem=x_recv.at[k],
+                dst_ref=rbuf.at[q, part], send_sem=x_send.at[k], recv_sem=x_recv.at[k, q],
                 device_id=partner, device_id_type=MESH).start()
 
     barrier = pltpu.get_barrier_semaphore()
@@ -181,26 +181,28 @@
         reduce_own(u)
 
     for k in range(CHUNKS):
-        arriving = rbuf.at[:, pl.ds(k * CX * YS, CX * YS)]
-        bytes_of(arriving, x_recv.at[k]).wait()
+        part = pl.ds(k * CX * YS, CX * YS)
         if k == 1:
             for u in range(CHUNKS):
                 forward(u)
         rows = pl.ds(k * CX, CX)
         acc[rows, :] = jnp.zeros((CX, HALF), F32)
 
-        def arrived(y, carry):
-            at = pl.ds(pl.multiple_of(y * LH, LH), LH)
-            cells = pl.ds(k * CX * YS + y, CX, stride=YS)
-            hi, lo = split(jnp.concatenate([rbuf[q, cells, :] for q in range(LH // 128)], axis=1))
-            rhi[rows, at] = hi
-            rlo[rows, at] = lo
-            mine = pl.ds(pl.multiple_of(n * COLS + y * LH, LH), LH)
-            ohi, olo = shi[:, mine], slo[:, mine]
+        for q in range(LH // 128):
+            bytes_of(rbuf.at[q, part], x_recv.at[k, q]).wait()
+            his, los, ohis, olos = [], [], [], []
+            for y in range(YS):
+                hi, lo = split(rbuf[q, pl.ds(k * CX * YS + y, CX, stride=YS), :])
+                at = pl.ds(y * LH + q * 128, 128)
+                rhi[rows, at] = hi
+                rlo[rows, at] = lo
+                mine = pl.ds(pl.multiple_of(n * COLS + y * LH + q * 128, 128), 128)
+                his.append(hi)
+                los.append(lo)
+                ohis.append(shi[:, mine])
+                olos.append(slo[:, mine])
+            hi, lo, ohi, olo = (jnp.concatenate(v, axis=1) for v in (his, los, ohis, olos))
             acc[rows, :] += dot_nt(hi, ohi) + (dot_nt(lo, ohi) + dot_nt(hi, olo))
-            return carry
-
-        lax.fori_loop(0, YS, arrived, 0)
         u = CHUNKS + k
         for h in range(2):
             stage[u, pl.ds(h * CX, CX), :] = acc[rows, pl.ds(h * 128, 128)]
@@ -281,11 +283,11 @@
         bytes_of(stage.at[u, fifteen], rs_send.at[u]).wait()
         pair_copy(u).wait_send()
         bytes_of(gathered.at[u, thirty], ag_send.at[u]).wait()
+    land_out = outs(core_land, other, land_sem)
     for b in range(2):
         core_copy(b).wait_recv()
-    land_out = outs(core_land, other, land_sem)
-    for copy in land_out:
-        copy.start()
+        for copy in land_out[b * (BL // 128) : (b + 1) * (BL // 128)]:
+            copy.start()
     for b in range(2):
         core_copy(b).wait_send()
     for copy in own_out + land_out:
@@ -316,7 +318,7 @@
             pltpu.VMEM((LH // 128, rows, 128), F32),
             pltpu.VMEM((LH // 128, rows, 128), F32),
             pltpu.VMEM((LH // 128, rows, 128), F32),
-            dma((LS // 128,)), dma((CHUNKS,)), dma((CHUNKS,)),
+            dma((LS // 128,)), dma((CHUNKS,)), dma((CHUNKS, LH // 128)),
             dma((UNITS,)), dma((UNITS,)), dma((UNITS,)), dma((UNITS,)), dma((UNITS,)), dma((UNITS,)),
             dma((2,)), dma((2,)), dma((LH // 128,)), dma((LH // 128,)),
         ],

time: 139 us -> 137 us (0.986)
  Pallas kernels: 137 us -> 135 us
    pallas_call x1, Pallas kernels: 137 us -> 135 us  [in_one_kernel(): pl.pallas_call(kernel, out_shape=jax.ShapeDtypeStruct((rows, LS), F32), i...]
where the time goes in v3:
time: 137 us
  Pallas kernels  135 us (99%)
  local copies, waits for them, and re-layouts  2 us (1%)
    pallas_call x1, Pallas kernels, in_one_kernel(): pl.pallas_call(kernel, out_shape=jax.ShapeDtypeStruct((rows, LS), F32), i...  135 us

profile of v3, /device:TPU:0, one launch (start us, length us, event | category | flops | bytes accessed | tf_op | source)
XLA Modules:
  0.0 137.3 jit_solution(10037384359936350606)
XLA Ops:
  0.0 1.0 copy.3.start_ref
  1.0 135.3 %shard_map.28 = f32[256,1024]{1,0:T(8,128)S(1)} custom-call(f32[2048,1024]{1,0:T(8,128)} %bitcast.3, f32[512,64]{1,0:T(8,128)S(1)} %copy.3.start_ref), custom_call_target="tpu_custom_call" | custom-call | tf_op jit(solution)/shard_map/pallas_call | solution.py:300
  136.4 1.0 copy.5
